TPU v7x, 32 devices: a whole 2x2x4 slice. The times are simulated.
32 devices in a mesh: dom: 4 (over x, core), st: 8 (over z, y).
Axes of the slice: x: 2, y: 2, z: 4, core: 2. Of those that a mesh axis runs over, the one named last changes fastest.
Arguments:
- orbitals: bfloat16 [512, 256, 1024], P('st', 'dom'), may hold values from -6 to 6
- potential: bfloat16 [256, 1024], P('dom'), may hold values from -0.5 to 0.5
- rotation: bfloat16 [512, 512], P('st'), may hold values from -0.25 to 0.25
Outputs:
- rotated: bfloat16 [512, 262144], P(None, ('dom', 'st'))
All inputs are finite; a program needn't handle non-finite values.
Results may differ from a plain program's by a relative error of at most 0.0049.
Values may be sent and summed in bfloat16 or wider, within the bound.
A program may use at most 128 MiB of HBM per device.

v0:
```python
import jax
import jax.numpy as jnp
from jax import lax
from jax.sharding import PartitionSpec as P

DEGREE = 4
NZ = 32


cheb_shift = 3.75
cheb_scale = 3.25


def extended(block, sides, width):
    for axis, dim in sides:
        count = lax.axis_size(axis)
        forward = [(i, i + 1) for i in range(count - 1)]
        backward = [(target, source) for source, target in forward]
        low = lax.ppermute(
            lax.slice_in_dim(block, block.shape[dim] - width, None, axis=dim), axis, forward
        )
        high = lax.ppermute(lax.slice_in_dim(block, 0, width, axis=dim), axis, backward)
        block = jnp.concatenate([low, block, high], axis=dim)
    return block


def neighbour_sum(center, nz_count):
    row_width = center.shape[2]
    z_position = lax.broadcasted_iota(jnp.int32, (1, 1, row_width), 2) % nz_count
    padded = jnp.pad(center, ((0, 0), (0, 0), (nz_count, nz_count)))
    along_y = padded[:, :, 2 * nz_count :] + padded[:, :, :row_width]
    upper_z = jnp.where(
        z_position < nz_count - 1, padded[:, :, nz_count + 1 : nz_count + 1 + row_width], 0.0
    )
    lower_z = jnp.where(z_position > 0, padded[:, :, nz_count - 1 : nz_count - 1 + row_width], 0.0)
    return along_y + upper_z + lower_z


def hamiltonian(padded_x, local_pot, nz_count):
    center = padded_x[:, 1:-1]
    beside = padded_x[:, 2:] + padded_x[:, :-2] + neighbour_sum(center, nz_count)
    return (3.0 + local_pot) * center - 0.5 * beside


def chebyshev(start, apply_fn, degree):
    previous = start
    current = (apply_fn(start) - cheb_shift * start) / cheb_scale
    for filter_order in range(1, degree):
        following = 2.0 * (apply_fn(current) - cheb_shift * current) / cheb_scale - previous
        previous = current
        current = following
    return current


def local(orbitals, potential, rotation):
    start = orbitals.astype(jnp.float32)
    local_pot = potential.astype(jnp.float32)
    states_dev, planes, row_width = start.shape

    def apply_step(state_field):
        padded = extended(state_field, (("dom", 1),), 1)
        return hamiltonian(padded, local_pot, NZ)

    result = chebyshev(start, apply_step, DEGREE)
    filtered = result.astype(jnp.bfloat16).reshape(states_dev, planes * row_width)
    regrouped = lax.all_to_all(filtered, "st", split_axis=1, concat_axis=0, tiled=True)
    product = jnp.dot(
        lax.all_gather(rotation, "st", axis=0, tiled=True),
        regrouped,
        preferred_element_type=jnp.float32,
    )
    return product.astype(jnp.bfloat16)


def solution(mesh):
    return jax.shard_map(
        local,
        mesh=mesh,
        in_specs=(P("st", "dom", None), P("dom", None), P("st", None)),
        out_specs=P(None, ("dom", "st")),
        check_vma=False,
    )
```

profile of v0, /device:TPU:0, one launch (start us, length us, event | category | flops | bytes accessed | tf_op | source)
XLA Modules:
  0.0 514.9 jit_solution(18047732025060596415)
XLA Ops:
  0.0 14.0 %copy_convert_fusion = f32[64,64,1024]{2,0,1:T(8,128)} fusion(bf16[64,64,1024]{2,1,0:T(8,128)(2,1)} %param.3), kind=kLoop, calls=%fused_computation.73 | loop fusion | flops 4194304 | bytes 25165824 | tf_op jit(solution)/shard_map/convert_element_type | solution.py:56
  14.0 1.2 fusion.57
  15.2 1.4 collective-permute-start
  16.7 3.0 collective-permute-start.1
  20.8 49.6 %broadcast_multiply_fusion = (f32[64,64,1024]{2,0,1:T(8,128)}, f32[64,64,1024]{2,0,1:T(8,128)}) fusion(f32[64,64,1024]{2,0,1:T(8,128)} %copy_convert_fusion, pred[1024]{0:T(1024)(128)(4,1)S(1)} %get-tuple-element.17, pred[1024]{0:T(1024)(128)(4,1)S(1)} %get-tuple-element.18, f32[64,1,1024]{2,0,1:T(8,128)S(1)} %collective-permute-done.1, ...), kind=kLoop, calls=%fused_computation.74 | loop fusion | flops 62914560 | bytes 51120128 | tf_op jit(solution)/shard_map/div | solution.py:47
  70.5 1.1 fusion.56
  71.5 1.3 collective-permute-start.2
  72.8 7.4 %collective-permute-start.3 = (f32[64,1,1024]{2,0,1:T(8,128)S(1)}, f32[64,1,1024]{2,0,1:T(8,128)S(1)}, u32[]{:S(2)}, u32[]{:S(2)}) collective-permute-start(f32[64,1,1024]{2,0,1:T(8,128)S(1)} %get-tuple-element.12), channel_id=1, source_target_pairs={{0,8},{8,16},{16,24},{1,9},{9,17},{17,25},{2,10},{10,18},{18,26},{... | collective-permute-start | bytes 786440 | tf_op jit(solution)/shard_map/ppermute | solution.py:19
  81.2 47.6 %fusion.17 = f32[64,64,1024]{2,0,1:T(8,128)} fusion(f32[64,64,1024]{2,0,1:T(8,128)} %get-tuple-element.5, f32[64,1,1024]{2,0,1:T(8,128)S(1)} %collective-permute-done.3, f32[64,1,1024]{2,0,1:T(8,128)S(1)} %collective-permute-done.2, f32[64,64,1024]{2,0,1:T(8,128)} %get-tuple-element.6, f32[64,1024]{1,0:T(8,128)S(1)} %get-tuple-element.15, ...), kind=kLoop, calls=%fused_computation.33 | loop fusion | flops 71303168 | bytes 59508736 | tf_op jit(solution)/shard_map/sub | solution.py:49
  128.8 1.1 fusion.55
  129.9 1.3 collective-permute-start.4
  131.2 7.2 %collective-permute-start.5 = (f32[64,1,1024]{2,0,1:T(8,128)S(1)}, f32[64,1,1024]{2,0,1:T(8,128)S(1)}, u32[]{:S(2)}, u32[]{:S(2)}) collective-permute-start(f32[64,1,1024]{2,0,1:T(8,128)S(1)} %get-tuple-element.10), channel_id=1, source_target_pairs={{0,8},{8,16},{16,24},{1,9},{9,17},{17,25},{2,10},{10,18},{18,26},{... | collective-permute-start | bytes 786440 | tf_op jit(solution)/shard_map/ppermute | solution.py:19
  138.4 1.1 collective-permute-done.5
  139.5 48.5 %fusion.28 = f32[64,64,1024]{2,0,1:T(8,128)} fusion(f32[64,64,1024]{2,0,1:T(8,128)} %fusion.17, f32[64,1,1024]{2,0,1:T(8,128)S(1)} %collective-permute-done.5, f32[64,1,1024]{2,0,1:T(8,128)S(1)} %collective-permute-done.4, f32[64,64,1024]{2,0,1:T(8,128)} %get-tuple-element.6, f32[64,1024]{1,0:T(8,128)S(1)} %get-tuple-element.16, ...), kind=kLoop, calls=%fused_computation.44 | loop fusion | flops 71303168 | bytes 51120128 | tf_op jit(solution)/shard_map/sub | solution.py:49
  189.0 1.3 collective-permute-start.6
  190.3 7.4 %collective-permute-start.7 = (f32[64,1,1024]{2,0,1:T(8,128)S(1)}, f32[64,1,1024]{2,0,1:T(8,128)S(1)}, u32[]{:S(2)}, u32[]{:S(2)}) collective-permute-start(f32[64,1,1024]{2,0,1:T(8,128)S(1)} %get-tuple-element.8), channel_id=1, source_target_pairs={{0,8},{8,16},{16,24},{1,9},{9,17},{17,25},{2,10},{10,18},{18,26},{... | collective-permute-start | bytes 786440 | tf_op jit(solution)/shard_map/ppermute | solution.py:19
  198.7 46.6 %fusion.40 = bf16[64,64,1024]{2,0,1:T(8,128)(2,1)} fusion(f32[64,64,1024]{2,0,1:T(8,128)} %fusion.17, f32[64,64,1024]{2,0,1:T(8,128)} %fusion.28, f32[64,1,1024]{2,0,1:T(8,128)S(1)} %collective-permute-done.7, f32[64,1,1024]{2,0,1:T(8,128)S(1)} %collective-permute-done.6, f32[64,1024]{1,0:T(8,128)S(1)} %get-tuple-element.16, ...), kind=kLoop, calls=%fused_computation.56 | loop fusion | flops 71303168 | bytes 42731520 | tf_op jit(solution)/shard_map/convert_element_type | solution.py:65
  245.3 11.3 %copy.9 = bf16[64,64,1024]{2,1,0:T(8,128)(2,1)} copy(bf16[64,64,1024]{2,0,1:T(8,128)(2,1)} %fusion.40) | data formatting | bytes 16777216 | tf_op jit(solution)/shard_map/convert_element_type | solution.py:65
  256.6 13.4 %all_to_all.14 = bf16[64,8,8192]{2,1,0:T(8,128)(2,1)} reshape(bf16[64,64,1024]{2,1,0:T(8,128)(2,1)} %copy.9) | data formatting | bytes 16777216 | tf_op jit(solution)/shard_map/all_to_all | solution.py:66
  270.0 11.2 %copy.10 = bf16[64,8,8192]{2,0,1:T(8,128)(2,1)} copy(bf16[64,8,8192]{2,1,0:T(8,128)(2,1)} %all_to_all.14) | data formatting | bytes 16777216 | tf_op jit(solution)/shard_map/all_to_all | solution.py:66
  281.3 5.8 %all-to-all-start = ((bf16[64,8,8192]{2,0,1:T(8,128)(2,1)}), bf16[64,8,8192]{2,0,1:T(8,128)(2,1)}, u32[]{:S(2)}, u32[]{:S(2)}) async-start(bf16[64,8,8192]{2,0,1:T(8,128)(2,1)} %copy.10), calls=%async_computation | async-start | bytes 16777216 | tf_op jit(solution)/shard_map/all_to_all | solution.py:66
  287.1 205.6 %all_gather.3 = bf16[512,512]{1,0:T(8,128)(2,1)S(1)} all-gather(bf16[64,512]{1,0:T(8,128)(2,1)S(1)} %copy-done.1), channel_id=1, replica_groups=mesh['dom'=4,'st'=8] {'st'}, dimensions={0}, use_global_device_ids=true | all-gather | bytes 589824 | tf_op jit(solution)/shard_map/all_gather | solution.py:68
  492.7 10.3 %fusion.47 = bf16[512,8192]{0,1:T(8,128)(2,1)} fusion(bf16[512,8192]{1,0:T(8,128)(2,1)} %bitcast.1, bf16[512,512]{1,0:T(8,128)(2,1)S(1)} %all_gather.3), kind=kOutput, calls=%fused_computation.72 | convolution fusion | flops 4299161600 | bytes 17301504 | tf_op jit(solution)/shard_map/dot_general | solution.py:67
  503.0 11.9 %copy.11 = bf16[512,8192]{1,0:T(8,128)(2,1)} copy(bf16[512,8192]{0,1:T(8,128)(2,1)} %fusion.47) | data formatting | bytes 16777216 | tf_op jit(solution)/shard_map/convert_element_type | solution.py:72
  (20 shorter events, 4.0 us)
Async XLA Ops:
  0.0 19.7 %copy-start = (bf16[64,1024]{1,0:T(8,128)(2,1)S(1)}, bf16[64,1024]{1,0:T(8,128)(2,1)}, u32[]{:S(2)}) copy-start(bf16[64,1024]{1,0:T(8,128)(2,1)} %param.4) | copy-start | bytes 393220
  14.0 67.2 %slice-start = ((s8[8388608]{0:T(1024)(128)(4,1)}), s8[4194304]{0:T(1024)(128)(4,1)S(1)}, s32[]{:S(2)}) async-start(s8[8388608]{0:T(1024)(128)(4,1)} %bitcast.7), calls=%async_computation.1 | async-start | bytes 8388608
  15.2 4.6 collective-permute-start
  16.7 4.2 collective-permute-start.1
  20.8 60.4 %slice-start.1 = ((s8[8388608]{0:T(1024)(128)(4,1)}), s8[4194304]{0:T(1024)(128)(4,1)S(1)}, s32[]{:S(2)}) async-start(s8[8388608]{0:T(1024)(128)(4,1)} %bitcast.7), calls=%async_computation.2 | async-start | bytes 8388608
  71.5 8.8 %collective-permute-start.2 = (f32[64,1,1024]{2,0,1:T(8,128)S(1)}, f32[64,1,1024]{2,0,1:T(8,128)S(1)}, u32[]{:S(2)}, u32[]{:S(2)}) collective-permute-start(f32[64,1,1024]{2,0,1:T(8,128)S(1)} %get-tuple-element.11), channel_id=1, source_target_pairs={{8,0},{16,8},{24,16},{9,1},{17,9},{25,17},{10,2},{18,10},{26,18},{... | collective-permute-start | bytes 786440 | tf_op jit(solution)/shard_map/ppermute | solution.py:22
  72.8 8.4 %collective-permute-start.3 = (f32[64,1,1024]{2,0,1:T(8,128)S(1)}, f32[64,1,1024]{2,0,1:T(8,128)S(1)}, u32[]{:S(2)}, u32[]{:S(2)}) collective-permute-start(f32[64,1,1024]{2,0,1:T(8,128)S(1)} %get-tuple-element.12), channel_id=1, source_target_pairs={{0,8},{8,16},{16,24},{1,9},{9,17},{17,25},{2,10},{10,18},{18,26},{... | collective-permute-start | bytes 786440 | tf_op jit(solution)/shard_map/ppermute | solution.py:19
  129.9 8.5 %collective-permute-start.4 = (f32[64,1,1024]{2,0,1:T(8,128)S(1)}, f32[64,1,1024]{2,0,1:T(8,128)S(1)}, u32[]{:S(2)}, u32[]{:S(2)}) collective-permute-start(f32[64,1,1024]{2,0,1:T(8,128)S(1)} %get-tuple-element.9), channel_id=1, source_target_pairs={{8,0},{16,8},{24,16},{9,1},{17,9},{25,17},{10,2},{18,10},{26,18},{... | collective-permute-start | bytes 786440 | tf_op jit(solution)/shard_map/ppermute | solution.py:22
  131.2 8.3 %collective-permute-start.5 = (f32[64,1,1024]{2,0,1:T(8,128)S(1)}, f32[64,1,1024]{2,0,1:T(8,128)S(1)}, u32[]{:S(2)}, u32[]{:S(2)}) collective-permute-start(f32[64,1,1024]{2,0,1:T(8,128)S(1)} %get-tuple-element.10), channel_id=1, source_target_pairs={{0,8},{8,16},{16,24},{1,9},{9,17},{17,25},{2,10},{10,18},{18,26},{... | collective-permute-start | bytes 786440 | tf_op jit(solution)/shard_map/ppermute | solution.py:19
  189.0 8.7 %collective-permute-start.6 = (f32[64,1,1024]{2,0,1:T(8,128)S(1)}, f32[64,1,1024]{2,0,1:T(8,128)S(1)}, u32[]{:S(2)}, u32[]{:S(2)}) collective-permute-start(f32[64,1,1024]{2,0,1:T(8,128)S(1)} %get-tuple-element.7), channel_id=1, source_target_pairs={{8,0},{16,8},{24,16},{9,1},{17,9},{25,17},{10,2},{18,10},{26,18},{... | collective-permute-start | bytes 786440 | tf_op jit(solution)/shard_map/ppermute | solution.py:22
  190.3 8.3 %collective-permute-start.7 = (f32[64,1,1024]{2,0,1:T(8,128)S(1)}, f32[64,1,1024]{2,0,1:T(8,128)S(1)}, u32[]{:S(2)}, u32[]{:S(2)}) collective-permute-start(f32[64,1,1024]{2,0,1:T(8,128)S(1)} %get-tuple-element.8), channel_id=1, source_target_pairs={{0,8},{8,16},{16,24},{1,9},{9,17},{17,25},{2,10},{10,18},{18,26},{... | collective-permute-start | bytes 786440 | tf_op jit(solution)/shard_map/ppermute | solution.py:19
  270.0 17.1 %copy-start.1 = (bf16[64,512]{1,0:T(8,128)(2,1)S(1)}, bf16[64,512]{1,0:T(8,128)(2,1)}, u32[]{:S(2)}) copy-start(bf16[64,512]{1,0:T(8,128)(2,1)} %param.5) | copy-start | bytes 196612
  281.3 211.4 %all-to-all-start = ((bf16[64,8,8192]{2,0,1:T(8,128)(2,1)}), bf16[64,8,8192]{2,0,1:T(8,128)(2,1)}, u32[]{:S(2)}, u32[]{:S(2)}) async-start(bf16[64,8,8192]{2,0,1:T(8,128)(2,1)} %copy.10), calls=%async_computation | async-start | bytes 16777216 | tf_op jit(solution)/shard_map/all_to_all | solution.py:66
where the time goes:
time: 516 us; the launch traced here: 515 us
  other arithmetic  206 us (40%)
  blocking collectives  206 us (40%)
  local copies, waits for them, and re-layouts  52.3 us (10%)
  starting transfers between devices  36.2 us (7%)
  matrix products  10.3 us (2%)
    all_gather x1, blocking collectives, local(): lax.all_gather(rotation, 'st', axis=0, tiled=True)  206 us
    sub x2, other arithmetic, chebyshev(): 2.0 * (apply_fn(current) - cheb_shift * current) / cheb_scale - previous  96 us
    div x1, other arithmetic, chebyshev(): current = (apply_fn(start) - cheb_shift * start) / cheb_scale  49.6 us
    convert_element_type x1, other arithmetic, local(): result.astype(jnp.bfloat16).reshape(states_dev, planes * row_width)  46.6 us
    ppermute x4, starting transfers between devices, extended(): lax.ppermute(lax.slice_in_dim(block, block.shape[dim] - width, None, axis...  25.1 us
    all_to_all x2, local copies, waits for them, and re-layouts, local(): lax.all_to_all(filtered, 'st', split_axis=1, concat_axis=0, tiled=True)  24.7 us
    convert_element_type x1, other arithmetic, local(): start = orbitals.astype(jnp.float32)  14 us
    convert_element_type x1, local copies, waits for them, and re-layouts, local(): return product.astype(jnp.bfloat16)  11.9 us
  transfers between devices with their start and end apart: 9, of which 4 were waited for; matrix products, arithmetic and copies ran while one was open for 0% of the time, Pallas kernels for 0%

commit v1 on v0

v1 whole, which is shorter than its diff:
```python
import functools

import jax
import jax.numpy as jnp
from jax import lax
from jax.experimental import pallas as pl
from jax.experimental.pallas import tpu as pltpu
from jax.sharding import PartitionSpec as P

DEGREE = 4
NZ = 32
LANES = 128
ROWS = 16
MESH = pl.DeviceIdType.MESH

cheb_shift = 3.75
cheb_scale = 3.25


def filter_kernel(
    n_dom, n_st, parts,
    orb, pot, rot,
    gathered, rot_full,
    raw, halo, pot_v, pot_halo, alpha, y0, y1, y2, y3, stage,
    load_sem, pot_sem, halo_send, halo_recv, ph_send, ph_recv,
    send_sem, recv_sem, own_sem, r_send, r_recv, r_own, r2_send, r2_recv,
):
    dom = lax.axis_index("dom")
    me = lax.axis_index("st")
    states, planes, width = orb.shape
    chunks = states // ROWS
    block = planes // n_st
    half = n_st // 2
    cols = width // LANES
    part_rows = states // parts
    fields = (y0, y1, y2, y3)

    def load(c):
        return pltpu.make_async_copy(
            orb.at[pl.ds(c * ROWS, ROWS)], raw.at[pl.ds(c * ROWS, ROWS)], load_sem.at[c]
        )

    for c in range(chunks):
        load(c).start()
    pot_copy = pltpu.make_async_copy(pot, pot_v, pot_sem)
    pot_copy.start()

    barrier = pltpu.get_barrier_semaphore()
    for i in range(1, n_st):
        pl.semaphore_signal(
            barrier, inc=1, device_id={"st": lax.rem(me + i, n_st)}, device_id_type=MESH
        )
    for i in range(1, n_dom):
        pl.semaphore_signal(
            barrier, inc=1, device_id={"dom": lax.rem(dom + i, n_dom)}, device_id_type=MESH
        )

    lane = lax.broadcasted_iota(jnp.int32, (ROWS, LANES), 1)
    z_pos = lane % NZ

    for field in fields:
        field[pl.ds(0, DEGREE)] = jnp.zeros((DEGREE, ROWS, width), jnp.float32)
        field[pl.ds(planes + DEGREE, DEGREE)] = jnp.zeros((DEGREE, ROWS, width), jnp.float32)

    pl.semaphore_wait(barrier, n_st - 1 + n_dom - 1)

    def halo_copy(side, c):
        begin = planes - ROWS if side == 0 else 0
        target = jnp.clip(dom + 1 if side == 0 else dom - 1, 0, n_dom - 1)
        return pltpu.make_async_remote_copy(
            src_ref=orb.at[pl.ds(c * ROWS, ROWS), pl.ds(begin, ROWS)],
            dst_ref=halo.at[side, c],
            send_sem=halo_send.at[side, c],
            recv_sem=halo_recv.at[side, c],
            device_id={"dom": target},
            device_id_type=MESH,
        )

    def pot_halo_copy(side):
        begin = planes - ROWS if side == 0 else 0
        target = jnp.clip(dom + 1 if side == 0 else dom - 1, 0, n_dom - 1)
        return pltpu.make_async_remote_copy(
            src_ref=pot.at[pl.ds(begin, ROWS)],
            dst_ref=pot_halo.at[side],
            send_sem=ph_send.at[side],
            recv_sem=ph_recv.at[side],
            device_id={"dom": target},
            device_id_type=MESH,
        )

    has_next = dom < n_dom - 1
    has_prev = dom > 0
    sends_side = (has_next, has_prev)
    takes_side = (has_prev, has_next)

    for side in range(2):
        @pl.when(sends_side[side])
        def _():
            pot_halo_copy(side).start()
            for c in range(chunks):
                halo_copy(side, c).start()

    part = dom if parts > 1 else 0
    my_rows = rot.at[pl.ds(pl.multiple_of(part * part_rows, ROWS), part_rows)]

    def rot_copy(i, owner):
        return pltpu.make_async_remote_copy(
            src_ref=my_rows,
            dst_ref=rot_full.at[owner, part],
            send_sem=r_send.at[i],
            recv_sem=r_recv.at[owner],
            device_id={"st": lax.rem(me + i, n_st)},
            device_id_type=MESH,
        )

    for i in range(1, n_st):
        rot_copy(i, me).start()
    rot_own = pltpu.make_async_copy(my_rows, rot_full.at[me, part], r_own)
    rot_own.start()

    def set_alpha(source, source_row, q):
        row = 2.0 * (source.astype(jnp.float32) - (cheb_shift - 3.0))
        for i in range(ROWS):
            if source_row[0] <= i < source_row[1]:
                alpha[q + i - source_row[0]] = jnp.broadcast_to(row[i : i + 1], (8, width))

    pot_copy.wait()

    def alpha_rows(j, carry):
        set_alpha(pot_v[pl.ds(pl.multiple_of(j * ROWS, ROWS), ROWS)], (0, ROWS), DEGREE + j * ROWS)
        return carry

    lax.fori_loop(0, planes // ROWS, alpha_rows, 0)

    def turned(value):
        return jnp.swapaxes(value.astype(jnp.float32), 0, 1)

    def advance(k, q, c, b):
        source = fields[k - 1]
        values = [source[q, :, pl.ds(i * LANES, LANES)] for i in range(cols)]
        ups = [pltpu.roll(v, LANES - NZ, 1) for v in values]
        downs = [pltpu.roll(v, NZ, 1) for v in values]
        zero = jnp.zeros((ROWS, LANES), jnp.float32)
        for i in range(cols):
            at = pl.ds(i * LANES, LANES)
            v = values[i]
            upper_z = jnp.where(z_pos < NZ - 1, pltpu.roll(v, LANES - 1, 1), 0.0)
            lower_z = jnp.where(z_pos > 0, pltpu.roll(v, 1, 1), 0.0)
            upper_y = jnp.where(lane < LANES - NZ, ups[i], ups[i + 1] if i + 1 < cols else zero)
            lower_y = jnp.where(lane >= NZ, downs[i], downs[i - 1] if i else zero)
            beside = (source[q + 1, :, at] + source[q - 1, :, at]) + (upper_y + lower_y)
            beside = beside + (upper_z + lower_z)
            a8 = alpha[q, :, at]
            applied = jnp.concatenate([a8] * (ROWS // 8), axis=0) * v - beside
            if k == 1:
                result = applied * (0.5 / cheb_scale)
            else:
                result = applied * (1.0 / cheb_scale) - fields[k - 2][q, :, at]
            if k < DEGREE:
                fields[k][q, :, at] = result
            else:
                offset = (q - DEGREE - b * block) * width + i * LANES
                stage[c, b, :, pl.ds(pl.multiple_of(offset, LANES), LANES)] = result.astype(
                    jnp.bfloat16
                )

    def send_copy(c, b):
        return pltpu.make_async_remote_copy(
            src_ref=stage.at[c, b],
            dst_ref=gathered.at[pl.ds(pl.multiple_of(me * states + c * ROWS, ROWS), ROWS)],
            send_sem=send_sem.at[c, b],
            recv_sem=recv_sem.at[c, me],
            device_id={"st": b},
            device_id_type=MESH,
        )

    def own_copy(c):
        return pltpu.make_async_copy(
            stage.at[c, me],
            gathered.at[pl.ds(pl.multiple_of(me * states + c * ROWS, ROWS), ROWS)],
            own_sem.at[c],
        )

    up_first = (me < half).astype(jnp.int32)
    halo_blocks = -(-DEGREE // block)

    def chunk_body(c, carry):
        load(c).wait()

        def turn(j, inner):
            at_planes = pl.ds(pl.multiple_of(j * ROWS, ROWS), ROWS)
            for i in range(cols):
                at = pl.ds(i * LANES, LANES)
                value = raw[pl.ds(pl.multiple_of(c * ROWS, ROWS), ROWS), at_planes, at]
                y0[pl.ds(DEGREE + j * ROWS, ROWS), :, at] = turned(value)
            return inner

        lax.fori_loop(0, planes // ROWS, turn, 0)

        def step_body(step, inner):
            in_first = (step < half).astype(jnp.int32)
            j = jnp.where(step < half, step, step - half)
            up = in_first * up_first + (1 - in_first) * (1 - up_first)
            b = up * (half + j) + (1 - up) * (half - 1 - j)

            for side in range(2):
                @pl.when((j == half - halo_blocks) & (up == side) & takes_side[side])
                def _():
                    halo_copy(side, c).wait_recv()
                    begin = ROWS - DEGREE if side == 0 else 0
                    q = 0 if side == 0 else planes + DEGREE
                    for i in range(cols):
                        at = pl.ds(i * LANES, LANES)
                        y0[pl.ds(q, DEGREE), :, at] = turned(halo[side, c, :, :, at])[
                            begin : begin + DEGREE
                        ]

                    @pl.when(c == 0)
                    def _():
                        pot_halo_copy(side).wait_recv()
                        set_alpha(pot_halo[side], (begin, begin + DEGREE), q)

            is_start = (step == 0).astype(jnp.int32)
            for k in range(1, DEGREE + 1):
                reach = DEGREE - k
                low = b * block + DEGREE - reach + 2 * reach * up * (1 - is_start)
                high = b * block + block + DEGREE - reach + 2 * reach * jnp.maximum(up, is_start)
                low = jnp.maximum(low, jnp.where(has_prev, k, DEGREE))
                high = jnp.minimum(
                    high, jnp.where(has_next, planes + DEGREE + reach, planes + DEGREE)
                )

                def plane_body(q, nothing):
                    advance(k, q, c, b)
                    return nothing

                lax.fori_loop(low, high, plane_body, 0)

            @pl.when(b != me)
            def _():
                send_copy(c, b).start()

            @pl.when(b == me)
            def _():
                own_copy(c).start()

            return inner

        lax.fori_loop(0, n_st, step_body, 0)
        return carry

    lax.fori_loop(0, chunks, chunk_body, 0)

    for i in range(1, n_st):
        rot_copy(i, lax.rem(me + i, n_st)).wait_recv()
    rot_own.wait()
    if parts > 1:
        def spread_copy(i, owner):
            return pltpu.make_async_remote_copy(
                src_ref=rot_full.at[:, owner],
                dst_ref=rot_full.at[:, owner],
                send_sem=r2_send.at[i],
                recv_sem=r2_recv.at[owner],
                device_id={"dom": lax.rem(dom + i, n_dom)},
                device_id_type=MESH,
            )

        for i in range(1, n_dom):
            spread_copy(i, dom).start()
        for i in range(1, n_dom):
            spread_copy(i, dom).wait_send()
            spread_copy(i, lax.rem(dom + i, n_dom)).wait_recv()
    for i in range(1, n_st):
        rot_copy(i, me).wait_send()
    for side in range(2):
        @pl.when(sends_side[side])
        def _():
            pot_halo_copy(side).wait_send()
            for c in range(chunks):
                halo_copy(side, c).wait_send()

    def arrival(c, i):
        peer = lax.rem(me + i, n_st)
        return pltpu.make_async_remote_copy(
            src_ref=stage.at[c, peer],
            dst_ref=gathered.at[pl.ds(pl.multiple_of(peer * states + c * ROWS, ROWS), ROWS)],
            send_sem=send_sem.at[c, peer],
            recv_sem=recv_sem.at[c, peer],
            device_id={"st": peer},
            device_id_type=MESH,
        )

    def finish(c, carry):
        def finish_peer(i, inner):
            arrival(c, i).wait_send()
            arrival(c, i).wait_recv()
            return inner

        lax.fori_loop(1, n_st, finish_peer, 0)
        own_copy(c).wait()
        return carry

    lax.fori_loop(0, chunks, finish, 0)


def rotate_kernel(rot, states, out):
    out[...] = jnp.dot(rot[...], states[...], preferred_element_type=jnp.float32).astype(out.dtype)


def local(n_dom, n_st, orbitals, potential, rotation):
    states, planes, width = orbitals.shape
    total = rotation.shape[1]
    chunks = states // ROWS
    block = planes // n_st
    points = block * width
    parts = n_dom if states % (ROWS * n_dom) == 0 else 1
    field = pltpu.VMEM((planes + 2 * DEGREE, ROWS, width), jnp.float32)
    dma = pltpu.SemaphoreType.DMA
    anywhere = pl.BlockSpec(memory_space=pl.ANY)
    gathered, rot_full = pl.pallas_call(
        functools.partial(filter_kernel, n_dom, n_st, parts),
        out_shape=(
            jax.ShapeDtypeStruct((n_st * states, points), jnp.bfloat16),
            jax.ShapeDtypeStruct((n_st, parts, states // parts, total), jnp.bfloat16),
        ),
        in_specs=[anywhere] * 3,
        out_specs=(anywhere, anywhere),
        scratch_shapes=[
            pltpu.VMEM((states, planes, width), jnp.bfloat16),
            pltpu.VMEM((2, chunks, ROWS, ROWS, width), jnp.bfloat16),
            pltpu.VMEM((planes, width), jnp.bfloat16),
            pltpu.VMEM((2, ROWS, width), jnp.bfloat16),
            pltpu.VMEM((planes + 2 * DEGREE, 8, width), jnp.float32),
            field, field, field, field,
            pltpu.VMEM((chunks, n_st, ROWS, points), jnp.bfloat16),
            dma((chunks,)), dma,
            dma((2, chunks)), dma((2, chunks)), dma((2,)), dma((2,)),
            dma((chunks, n_st)), dma((chunks, n_st)), dma((chunks,)),
            dma((n_st,)), dma((n_st,)), dma,
            dma((n_dom,)), dma((n_dom,)),
        ],
        compiler_params=pltpu.CompilerParams(
            collective_id=0, has_side_effects=True, vmem_limit_bytes=56 * 1024 * 1024
        ),
        cost_estimate=pl.CostEstimate(
            flops=13 * DEGREE * states * planes * width,
            bytes_accessed=4 * states * planes * width,
            transcendentals=0,
        ),
        name="filter_exchange",
    )(orbitals, potential, rotation)
    rot_all = rot_full.reshape(n_st * states, total)
    return pl.pallas_call(
        rotate_kernel,
        out_shape=jax.ShapeDtypeStruct((n_st * states, points), jnp.bfloat16),
        grid=(points // width,),
        in_specs=[
            pl.BlockSpec((n_st * states, total), lambda i: (0, 0)),
            pl.BlockSpec((n_st * states, width), lambda i: (0, i)),
        ],
        out_specs=pl.BlockSpec((n_st * states, width), lambda i: (0, i)),
        compiler_params=pltpu.CompilerParams(vmem_limit_bytes=32 * 1024 * 1024),
        cost_estimate=pl.CostEstimate(
            flops=2 * n_st * states * total * points,
            bytes_accessed=4 * n_st * states * points,
            transcendentals=0,
        ),
        name="rotate",
    )(rot_all, gathered)


def solution(mesh):
    return jax.shard_map(
        functools.partial(local, mesh.shape["dom"], mesh.shape["st"]),
        mesh=mesh,
        in_specs=(P("st", "dom", None), P("dom", None), P("st", None)),
        out_specs=P(None, ("dom", "st")),
        check_vma=False,
    )
```

time: 516 us -> 217 us (0.42)
  Pallas kernels: 0 us -> 212 us
  other arithmetic: 206 us -> 0 us
  blocking collectives: 206 us -> 0 us
  local copies, waits for them, and re-layouts: 52.3 us -> 4.42 us
  starting transfers between devices: 36.2 us -> 0 us
  matrix products: 10.3 us -> 0 us
    pallas_call x0 -> x2, Pallas kernels: none -> 212 us  [the longest x1 204 us: local(): pl.pallas_call(functools.partial(filter_kernel, n_dom, n_st, parts), out_...]
    all_gather x1 -> x0, blocking collectives: 206 us -> none  [local(): lax.all_gather(rotation, 'st', axis=0, tiled=True)]
    sub x2 -> x0, other arithmetic: 96 us -> none  [chebyshev(): 2.0 * (apply_fn(current) - cheb_shift * current) / cheb_scale - previous]
    convert_element_type x2 -> x0, other arithmetic: 60.6 us -> none  [the longest x1 46.6 us: local(): result.astype(jnp.bfloat16).reshape(states_dev, planes * row_width)]
    div x1 -> x0, other arithmetic: 49.6 us -> none  [chebyshev(): current = (apply_fn(start) - cheb_shift * start) / cheb_scale]
    ppermute x8 -> x0, starting transfers between devices: 30.4 us -> none  [the longest x4 25.1 us: extended(): lax.ppermute(lax.slice_in_dim(block, block.shape[dim] - width, None, axis...]
    all_to_all x2 -> x0, local copies, waits for them, and re-layouts: 24.7 us -> none  [local(): lax.all_to_all(filtered, 'st', split_axis=1, concat_axis=0, tiled=True)]
    convert_element_type x2 -> x0, local copies, waits for them, and re-layouts: 23.3 us -> none  [the longest x1 11.9 us: local(): return product.astype(jnp.bfloat16)]
  transfers between devices with their start and end apart: 9 -> 0, of which waited for: 4 -> 0; matrix products, arithmetic and copies ran while one was open for 0% -> 0% of each run, Pallas kernels for 0% -> 0%
where the time goes in v1:
time: 217 us
  Pallas kernels  212 us (98%)
  local copies, waits for them, and re-layouts  4.42 us (2%)
    pallas_call x1, Pallas kernels, local(): pl.pallas_call(functools.partial(filter_kernel, n_dom, n_st, parts), out_...  204 us
    pallas_call x1, Pallas kernels, local(): pl.pallas_call(rotate_kernel, out_shape=jax.ShapeDtypeStruct((n_st * stat...  7.82 us
    unnamed x4, local copies, waits for them, and re-layouts  4.42 us

profile of v1, /device:TPU:0, one launch (start us, length us, event | category | flops | bytes accessed | tf_op | source)
XLA Modules:
  0.0 216.5 jit_solution(3713674091442212450)
XLA Ops:
  0.0 204.3 %filter_exchange.1 = (bf16[512,8192]{1,0:T(8,128)(2,1)}, bf16[8,4,16,512]{3,2,1,0:T(8,128)(2,1)}) custom-call(bf16[64,64,1024]{2,1,0:T(8,128)(2,1)} %orb.1, bf16[64,1024]{1,0:T(8,128)(2,1)} %pot.1, bf16[64,512]{1,0:T(8,128)(2,1)} %rot.1), custom_call_target="tpu_custom_call" | custom-call | flops 218103808 | bytes 16777216 | tf_op jit(solution)/shard_map/filter_exchange/pallas_call | solution.py:320
  204.3 0.0 copy-start
  204.3 3.4 %copy-done = bf16[512,8192]{1,0:T(8,128)(2,1)S(1)} copy-done((bf16[512,8192]{1,0:T(8,128)(2,1)S(1)}, bf16[512,8192]{1,0:T(8,128)(2,1)}, u32[]{:S(2)}) %copy-start) | copy-done | bytes 8388632
  207.7 0.0 copy-start.1
  207.7 1.0 copy-done.1
  208.7 7.8 %rotate.1 = bf16[512,8192]{1,0:T(8,128)(2,1)} custom-call(bf16[512,512]{1,0:T(8,128)(2,1)S(1)} %bitcast.1, bf16[512,8192]{1,0:T(8,128)(2,1)S(1)} %copy-done), custom_call_target="tpu_custom_call" | custom-call | flops 4294967296 | bytes 16777216 | tf_op jit(solution)/shard_map/rotate/pallas_call | solution.py:353
Async XLA Ops:
  204.3 3.4 %copy-start = (bf16[512,8192]{1,0:T(8,128)(2,1)S(1)}, bf16[512,8192]{1,0:T(8,128)(2,1)}, u32[]{:S(2)}) copy-start(bf16[512,8192]{1,0:T(8,128)(2,1)} %get-tuple-element.8.states) | copy-start | bytes 25165828
  207.7 1.0 copy-start.1

commit v2 on v1

--- a/solution.py
+++ b/solution.py
@@ -181,8 +181,26 @@
             own_sem.at[c],
         )
 
-    up_first = (me < half).astype(jnp.int32)
+    up_first = me < half
+    odd = lax.rem(me, 2) if half > 1 else 0
+    even = 1 - odd if half > 1 else 0
+    pivot = jnp.where(up_first, half + odd, half - 1 - even)
     halo_blocks = -(-DEGREE // block)
+    last = chunks - 1
+
+    def block_at(step):
+        upper = jnp.where(step < n_st - pivot, pivot + step, n_st - 1 - step)
+        lower = jnp.where(step <= pivot, pivot - step, step)
+        return jnp.where(up_first, upper, lower)
+
+    def issue(c, b):
+        @pl.when(b != me)
+        def _():
+            send_copy(c, b).start()
+
+        @pl.when(b == me)
+        def _():
+            own_copy(c).start()
 
     def chunk_body(c, carry):
         load(c).wait()
@@ -195,16 +213,29 @@
                 y0[pl.ds(DEGREE + j * ROWS, ROWS), :, at] = turned(value)
             return inner
 
-        lax.fori_loop(0, planes // ROWS, turn, 0)
+        begin_row = jnp.maximum(pivot * block - DEGREE, 0) // ROWS
+        end_row = jnp.minimum((pivot * block + block + DEGREE - 1) // ROWS + 1, planes // ROWS)
 
         def step_body(step, inner):
-            in_first = (step < half).astype(jnp.int32)
-            j = jnp.where(step < half, step, step - half)
-            up = in_first * up_first + (1 - in_first) * (1 - up_first)
-            b = up * (half + j) + (1 - up) * (half - 1 - j)
+            b = block_at(step)
+            up = jnp.where(
+                up_first, (step < n_st - pivot).astype(jnp.int32), (step > pivot).astype(jnp.int32)
+            )
+            is_start = (step == 0).astype(jnp.int32)
+
+            @pl.when(step == 0)
+            def _():
+                lax.fori_loop(begin_row, end_row, turn, 0)
+
+            @pl.when(step == 1)
+            def _():
+                lax.fori_loop(0, begin_row, turn, 0)
+                lax.fori_loop(end_row, planes // ROWS, turn, 0)
 
             for side in range(2):
-                @pl.when((j == half - halo_blocks) & (up == side) & takes_side[side])
+                needed = n_st - halo_blocks if side else halo_blocks - 1
+
+                @pl.when((b == needed) & (up == side) & takes_side[side])
                 def _():
                     halo_copy(side, c).wait_recv()
                     begin = ROWS - DEGREE if side == 0 else 0
@@ -220,7 +251,6 @@
                         pot_halo_copy(side).wait_recv()
                         set_alpha(pot_halo[side], (begin, begin + DEGREE), q)
 
-            is_start = (step == 0).astype(jnp.int32)
             for k in range(1, DEGREE + 1):
                 reach = DEGREE - k
                 low = b * block + DEGREE - reach + 2 * reach * up * (1 - is_start)
@@ -236,13 +266,21 @@
 
                 lax.fori_loop(low, high, plane_body, 0)
 
-            @pl.when(b != me)
-            def _():
-                send_copy(c, b).start()
-
-            @pl.when(b == me)
-            def _():
-                own_copy(c).start()
+            if chunks == 1:
+                issue(c, b)
+            else:
+                @pl.when((step < half) & (c > 0))
+                def _():
+                    issue(c - 1, block_at(step + half))
+
+                @pl.when((step < half) & (c < last))
+                def _():
+                    issue(c, b)
+
+                @pl.when((step >= half) & (c == last))
+                def _():
+                    issue(c, b)
+                    issue(c, block_at(step - half))
 
             return inner
 
@@ -359,7 +397,7 @@
             pl.BlockSpec((n_st * states, width), lambda i: (0, i)),
         ],
         out_specs=pl.BlockSpec((n_st * states, width), lambda i: (0, i)),
-        compiler_params=pltpu.CompilerParams(vmem_limit_bytes=32 * 1024 * 1024),
+        compiler_params=pltpu.CompilerParams(vmem_limit_bytes=60 * 1024 * 1024),
         cost_estimate=pl.CostEstimate(
             flops=2 * n_st * states * total * points,
             bytes_accessed=4 * n_st * states * points,

time: 217 us -> 212 us (0.977)
  local copies, waits for them, and re-layouts: 4.42 us -> 0 us
    unnamed x4 -> x0, local copies, waits for them, and re-layouts: 4.42 us -> none
    pallas_call x1, Pallas kernels: 204 us -> 201 us  [local(): pl.pallas_call(functools.partial(filter_kernel, n_dom, n_st, parts), out_...]
    pallas_call x1, Pallas kernels: 7.82 us -> 11 us  [local(): pl.pallas_call(rotate_kernel, out_shape=jax.ShapeDtypeStruct((n_st * stat...]
where the time goes in v2:
time: 212 us
  Pallas kernels  212 us (100%)
    pallas_call x1, Pallas kernels, local(): pl.pallas_call(functools.partial(filter_kernel, n_dom, n_st, parts), out_...  201 us
    pallas_call x1, Pallas kernels, local(): pl.pallas_call(rotate_kernel, out_shape=jax.ShapeDtypeStruct((n_st * stat...  11 us

profile of v2, /device:TPU:0, one launch (start us, length us, event | category | flops | bytes accessed | tf_op | source)
XLA Modules:
  0.0 211.8 jit_solution(10333805253054190197)
XLA Ops:
  0.0 200.8 %filter_exchange.1 = (bf16[512,8192]{1,0:T(8,128)(2,1)}, bf16[8,4,16,512]{3,2,1,0:T(8,128)(2,1)}) custom-call(bf16[64,64,1024]{2,1,0:T(8,128)(2,1)} %orb.1, bf16[64,1024]{1,0:T(8,128)(2,1)} %pot.1, bf16[64,512]{1,0:T(8,128)(2,1)} %rot.1), custom_call_target="tpu_custom_call" | custom-call | flops 218103808 | bytes 16777216 | tf_op jit(solution)/shard_map/filter_exchange/pallas_call | solution.py:358
  200.8 11.0 %rotate.1 = bf16[512,8192]{1,0:T(8,128)(2,1)} custom-call(bf16[512,512]{1,0:T(8,128)(2,1)} %bitcast.1, bf16[512,8192]{1,0:T(8,128)(2,1)} %get-tuple-element.8.states), custom_call_target="tpu_custom_call" | custom-call | flops 4294967296 | bytes 16777216 | tf_op jit(solution)/shard_map/rotate/pallas_call | solution.py:391

commit v3 on v2

--- a/solution.py
+++ b/solution.py
@@ -20,20 +20,24 @@
 def filter_kernel(
     n_dom, n_st, parts,
     orb, pot, rot,
-    gathered, rot_full,
-    raw, halo, pot_v, pot_halo, alpha, y0, y1, y2, y3, stage,
+    rotated1, gathered2, rot_full,
+    raw, halo, pot_v, pot_halo, alpha, y0, y1, y2, y3, stage1, stage2, gathered1, rot_v, turn_out,
     load_sem, pot_sem, halo_send, halo_recv, ph_send, ph_recv,
-    send_sem, recv_sem, own_sem, r_send, r_recv, r_own, r2_send, r2_recv,
+    send_sem, recv_sem, own_sem, r_send, r_recv, r_own, r2_send, r2_recv, out_sem,
 ):
     dom = lax.axis_index("dom")
     me = lax.axis_index("st")
     states, planes, width = orb.shape
     chunks = states // ROWS
     block = planes // n_st
+    late = gathered2.shape[1] // width
+    early = block - late
     half = n_st // 2
     cols = width // LANES
     part_rows = states // parts
     fields = (y0, y1, y2, y3)
+    stages = (stage1, stage2)
+    gathers = (gathered1, gathered2)
 
     def load(c):
         return pltpu.make_async_copy(
@@ -135,7 +139,7 @@
     def turned(value):
         return jnp.swapaxes(value.astype(jnp.float32), 0, 1)
 
-    def advance(k, q, c, b):
+    def advance(k, q, c, b, piece):
         source = fields[k - 1]
         values = [source[q, :, pl.ds(i * LANES, LANES)] for i in range(cols)]
         ups = [pltpu.roll(v, LANES - NZ, 1) for v in values]
@@ -159,26 +163,27 @@
             if k < DEGREE:
                 fields[k][q, :, at] = result
             else:
-                offset = (q - DEGREE - b * block) * width + i * LANES
-                stage[c, b, :, pl.ds(pl.multiple_of(offset, LANES), LANES)] = result.astype(
+                offset = (q - DEGREE - b * block - piece * early) * width + i * LANES
+                stages[piece][c, b, :, pl.ds(pl.multiple_of(offset, LANES), LANES)] = result.astype(
                     jnp.bfloat16
                 )
 
-    def send_copy(c, b):
+    def rows_of(owner, c):
+        return pl.ds(pl.multiple_of(owner * states + c * ROWS, ROWS), ROWS)
+
+    def send_copy(piece, c, b):
         return pltpu.make_async_remote_copy(
-            src_ref=stage.at[c, b],
-            dst_ref=gathered.at[pl.ds(pl.multiple_of(me * states + c * ROWS, ROWS), ROWS)],
-            send_sem=send_sem.at[c, b],
-            recv_sem=recv_sem.at[c, me],
+            src_ref=stages[piece].at[c, b],
+            dst_ref=gathers[piece].at[rows_of(me, c)],
+            send_sem=send_sem.at[piece, c, b],
+            recv_sem=recv_sem.at[piece, c, me],
             device_id={"st": b},
             device_id_type=MESH,
         )
 
-    def own_copy(c):
+    def own_copy(piece, c):
         return pltpu.make_async_copy(
-            stage.at[c, me],
-            gathered.at[pl.ds(pl.multiple_of(me * states + c * ROWS, ROWS), ROWS)],
-            own_sem.at[c],
+            stages[piece].at[c, me], gathers[piece].at[rows_of(me, c)], own_sem.at[piece, c]
         )
 
     up_first = me < half
@@ -193,14 +198,14 @@
         lower = jnp.where(step <= pivot, pivot - step, step)
         return jnp.where(up_first, upper, lower)
 
-    def issue(c, b):
+    def issue(piece, c, b):
         @pl.when(b != me)
         def _():
-            send_copy(c, b).start()
+            send_copy(piece, c, b).start()
 
         @pl.when(b == me)
         def _():
-            own_copy(c).start()
+            own_copy(piece, c).start()
 
     def chunk_body(c, carry):
         load(c).wait()
@@ -260,27 +265,30 @@
                     high, jnp.where(has_next, planes + DEGREE + reach, planes + DEGREE)
                 )
 
-                def plane_body(q, nothing):
-                    advance(k, q, c, b)
+                def plane_body(piece, q, nothing):
+                    advance(k, q, c, b, piece)
                     return nothing
 
-                lax.fori_loop(low, high, plane_body, 0)
+                cut = b * block + DEGREE + early if k == DEGREE else high
+                lax.fori_loop(low, cut, functools.partial(plane_body, 0), 0)
+                if k == DEGREE:
+                    lax.fori_loop(cut, high, functools.partial(plane_body, 1), 0)
 
             if chunks == 1:
-                issue(c, b)
+                issue(0, c, b)
             else:
                 @pl.when((step < half) & (c > 0))
                 def _():
-                    issue(c - 1, block_at(step + half))
+                    issue(0, c - 1, block_at(step + half))
 
                 @pl.when((step < half) & (c < last))
                 def _():
-                    issue(c, b)
+                    issue(0, c, b)
 
                 @pl.when((step >= half) & (c == last))
                 def _():
-                    issue(c, b)
-                    issue(c, block_at(step - half))
+                    issue(0, c, b)
+                    issue(0, c, block_at(step - half))
 
             return inner
 
@@ -288,6 +296,14 @@
         return carry
 
     lax.fori_loop(0, chunks, chunk_body, 0)
+
+    def late_body(t, carry):
+        c, j = t // half, lax.rem(t, half)
+        issue(1, c, block_at(j + half))
+        issue(1, c, block_at(j))
+        return carry
+
+    lax.fori_loop(0, chunks * half, late_body, 0)
 
     for i in range(1, n_st):
         rot_copy(i, lax.rem(me + i, n_st)).wait_recv()
@@ -317,32 +333,99 @@
             for c in range(chunks):
                 halo_copy(side, c).wait_send()
 
-    def arrival(c, i):
+    rot_load = pltpu.make_async_copy(rot_full, rot_v, r_own)
+    rot_load.start()
+    rot_load.wait()
+
+    def arrival(piece, c, i):
         peer = lax.rem(me + i, n_st)
         return pltpu.make_async_remote_copy(
-            src_ref=stage.at[c, peer],
-            dst_ref=gathered.at[pl.ds(pl.multiple_of(peer * states + c * ROWS, ROWS), ROWS)],
-            send_sem=send_sem.at[c, peer],
-            recv_sem=recv_sem.at[c, peer],
+            src_ref=stages[piece].at[c, peer],
+            dst_ref=gathers[piece].at[rows_of(peer, c)],
+            send_sem=send_sem.at[piece, c, peer],
+            recv_sem=recv_sem.at[piece, c, peer],
             device_id={"st": peer},
             device_id_type=MESH,
         )
 
-    def finish(c, carry):
+    def finish(piece, c, carry):
         def finish_peer(i, inner):
-            arrival(c, i).wait_send()
-            arrival(c, i).wait_recv()
+            arrival(piece, c, i).wait_send()
+            arrival(piece, c, i).wait_recv()
             return inner
 
         lax.fori_loop(1, n_st, finish_peer, 0)
-        own_copy(c).wait()
+        own_copy(piece, c).wait()
         return carry
 
-    lax.fori_loop(0, chunks, finish, 0)
-
-
-def rotate_kernel(rot, states, out):
-    out[...] = jnp.dot(rot[...], states[...], preferred_element_type=jnp.float32).astype(out.dtype)
+    lax.fori_loop(0, chunks, functools.partial(finish, 0), 0)
+
+    def columns(tile):
+        return pl.ds(pl.multiple_of(tile * width, width), width)
+
+    def out_copy(slot, tile):
+        return pltpu.make_async_copy(
+            turn_out.at[slot], rotated1.at[:, columns(tile)], out_sem.at[slot]
+        )
+
+    def rotate_tile(tile, carry):
+        slot = lax.rem(tile, 2)
+
+        @pl.when(tile >= 2)
+        def _():
+            out_copy(slot, tile - 2).wait()
+
+        rows = n_st * states
+        turn_out[slot] = jnp.dot(
+            rot_v[...].reshape(rows, rows),
+            gathered1[:, columns(tile)],
+            preferred_element_type=jnp.float32,
+        ).astype(jnp.bfloat16)
+        out_copy(slot, tile).start()
+        return carry
+
+    lax.fori_loop(0, early, rotate_tile, 0)
+    for tile in range(max(early - 2, 0), early):
+        out_copy(tile % 2, tile).wait()
+
+    lax.fori_loop(0, chunks, functools.partial(finish, 1), 0)
+
+
+def rotate_kernel(rot, gathered, rotated1, out, rot_v, held, result, in_sem, copy_sem, out_sem):
+    total, points = gathered.shape
+    tiles = held.shape[0]
+    width = points // tiles
+    done = rotated1.shape[1]
+    pieces = copy_sem.shape[0]
+    loads = [pltpu.make_async_copy(rot, rot_v, in_sem.at[tiles])]
+    for t in range(tiles):
+        loads.append(
+            pltpu.make_async_copy(
+                gathered.at[:, pl.ds(t * width, width)], held.at[t], in_sem.at[t]
+            )
+        )
+    copies = []
+    for i in range(pieces):
+        rows = pl.ds(i * (total // pieces), total // pieces)
+        copies.append(
+            pltpu.make_async_copy(rotated1.at[rows], out.at[rows, pl.ds(0, done)], copy_sem.at[i])
+        )
+    for copy in loads + copies:
+        copy.start()
+    loads[0].wait()
+    stores = []
+    for t in range(tiles):
+        loads[t + 1].wait()
+        result[t] = jnp.dot(
+            rot_v[...], held[t], preferred_element_type=jnp.float32
+        ).astype(out.dtype)
+        store = pltpu.make_async_copy(
+            result.at[t], out.at[:, pl.ds(done + t * width, width)], out_sem.at[t]
+        )
+        store.start()
+        stores.append(store)
+    for copy in copies + stores:
+        copy.wait()
 
 
 def local(n_dom, n_st, orbitals, potential, rotation):
@@ -350,19 +433,23 @@
     total = rotation.shape[1]
     chunks = states // ROWS
     block = planes // n_st
+    late = max(block // 4, 1)
     points = block * width
+    early_points = (block - late) * width
+    late_points = late * width
     parts = n_dom if states % (ROWS * n_dom) == 0 else 1
     field = pltpu.VMEM((planes + 2 * DEGREE, ROWS, width), jnp.float32)
     dma = pltpu.SemaphoreType.DMA
     anywhere = pl.BlockSpec(memory_space=pl.ANY)
-    gathered, rot_full = pl.pallas_call(
+    rotated1, gathered2, rot_full = pl.pallas_call(
         functools.partial(filter_kernel, n_dom, n_st, parts),
         out_shape=(
-            jax.ShapeDtypeStruct((n_st * states, points), jnp.bfloat16),
+            jax.ShapeDtypeStruct((n_st * states, early_points), jnp.bfloat16),
+            jax.ShapeDtypeStruct((n_st * states, late_points), jnp.bfloat16),
             jax.ShapeDtypeStruct((n_st, parts, states // parts, total), jnp.bfloat16),
         ),
         in_specs=[anywhere] * 3,
-        out_specs=(anywhere, anywhere),
+        out_specs=(anywhere,) * 3,
         scratch_shapes=[
             pltpu.VMEM((states, planes, width), jnp.bfloat16),
             pltpu.VMEM((2, chunks, ROWS, ROWS, width), jnp.bfloat16),
@@ -370,15 +457,19 @@
             pltpu.VMEM((2, ROWS, width), jnp.bfloat16),
             pltpu.VMEM((planes + 2 * DEGREE, 8, width), jnp.float32),
             field, field, field, field,
-            pltpu.VMEM((chunks, n_st, ROWS, points), jnp.bfloat16),
+            pltpu.VMEM((chunks, n_st, ROWS, early_points), jnp.bfloat16),
+            pltpu.VMEM((chunks, n_st, ROWS, late_points), jnp.bfloat16),
+            pltpu.VMEM((n_st * states, early_points), jnp.bfloat16),
+            pltpu.VMEM((n_st, parts, states // parts, total), jnp.bfloat16),
+            pltpu.VMEM((2, n_st * states, width), jnp.bfloat16),
             dma((chunks,)), dma,
             dma((2, chunks)), dma((2, chunks)), dma((2,)), dma((2,)),
-            dma((chunks, n_st)), dma((chunks, n_st)), dma((chunks,)),
+            dma((2, chunks, n_st)), dma((2, chunks, n_st)), dma((2, chunks)),
             dma((n_st,)), dma((n_st,)), dma,
-            dma((n_dom,)), dma((n_dom,)),
+            dma((n_dom,)), dma((n_dom,)), dma((2,)),
         ],
         compiler_params=pltpu.CompilerParams(
-            collective_id=0, has_side_effects=True, vmem_limit_bytes=56 * 1024 * 1024
+            collective_id=0, has_side_effects=True, vmem_limit_bytes=58 * 1024 * 1024
         ),
         cost_estimate=pl.CostEstimate(
             flops=13 * DEGREE * states * planes * width,
@@ -387,24 +478,27 @@
         ),
         name="filter_exchange",
     )(orbitals, potential, rotation)
-    rot_all = rot_full.reshape(n_st * states, total)
+    rows = n_st * states
+    pieces = 4
     return pl.pallas_call(
         rotate_kernel,
-        out_shape=jax.ShapeDtypeStruct((n_st * states, points), jnp.bfloat16),
-        grid=(points // width,),
-        in_specs=[
-            pl.BlockSpec((n_st * states, total), lambda i: (0, 0)),
-            pl.BlockSpec((n_st * states, width), lambda i: (0, i)),
+        out_shape=jax.ShapeDtypeStruct((rows, points), jnp.bfloat16),
+        in_specs=[anywhere] * 3,
+        out_specs=anywhere,
+        scratch_shapes=[
+            pltpu.VMEM((rows, total), jnp.bfloat16),
+            pltpu.VMEM((late, rows, width), jnp.bfloat16),
+            pltpu.VMEM((late, rows, width), jnp.bfloat16),
+            dma((late + 1,)), dma((pieces,)), dma((late,)),
         ],
-        out_specs=pl.BlockSpec((n_st * states, width), lambda i: (0, i)),
         compiler_params=pltpu.CompilerParams(vmem_limit_bytes=60 * 1024 * 1024),
         cost_estimate=pl.CostEstimate(
-            flops=2 * n_st * states * total * points,
-            bytes_accessed=4 * n_st * states * points,
+            flops=2 * rows * total * late_points,
+            bytes_accessed=4 * rows * points,
             transcendentals=0,
         ),
         name="rotate",
-    )(rot_all, gathered)
+    )(rot_full.reshape(rows, total), gathered2, rotated1)
 
 
 def solution(mesh):

time: 212 us -> 423 us (2.00)
  Pallas kernels: 212 us -> 423 us
    pallas_call x1, Pallas kernels: 11 us -> 192 us  [local(): pl.pallas_call(rotate_kernel, out_shape=jax.ShapeDtypeStruct((rows, point...]
    pallas_call x1, Pallas kernels: 201 us -> 231 us  [local(): pl.pallas_call(functools.partial(filter_kernel, n_dom, n_st, parts), out_...]
where the time goes in v3:
time: 423 us
  Pallas kernels  423 us (100%)
    pallas_call x1, Pallas kernels, local(): pl.pallas_call(functools.partial(filter_kernel, n_dom, n_st, parts), out_...  231 us
    pallas_call x1, Pallas kernels, local(): pl.pallas_call(rotate_kernel, out_shape=jax.ShapeDtypeStruct((rows, point...  192 us

profile of v3, /device:TPU:0, one launch (start us, length us, event | category | flops | bytes accessed | tf_op | source)
XLA Modules:
  0.0 422.6 jit_solution(4582392257031803860)
XLA Ops:
  0.0 230.8 %filter_exchange.1 = (bf16[512,6144]{1,0:T(8,128)(2,1)}, bf16[512,2048]{1,0:T(8,128)(2,1)}, bf16[8,4,16,512]{3,2,1,0:T(8,128)(2,1)}) custom-call(bf16[64,64,1024]{2,1,0:T(8,128)(2,1)} %orb.1, bf16[64,1024]{1,0:T(8,128)(2,1)} %pot.1, bf16[64,512]{1,0:T(8,128)(2,1)} %rot.1), custom_call_target="tpu_custom_call" | custom-call | flops 218103808 | bytes 16777216 | tf_op jit(solution)/shard_map/filter_exchange/pallas_call | solution.py:444
  230.8 191.8 %rotate.1 = bf16[512,8192]{1,0:T(8,128)(2,1)} custom-call(bf16[512,512]{1,0:T(8,128)(2,1)} %bitcast.1, bf16[512,2048]{1,0:T(8,128)(2,1)} %get-tuple-element.9.gathered, bf16[512,6144]{1,0:T(8,128)(2,1)} %get-tuple-element.10.rotated1), custom_call_target="tpu_custom_call" | custom-call | flops 1073741824 | bytes 16777216 | tf_op jit(solution)/shard_map/rotate/pallas_call | solution.py:483

commit v4 on v2

--- a/solution.py
+++ b/solution.py
@@ -11,6 +11,7 @@
 NZ = 32
 LANES = 128
 ROWS = 16
+GROUP = 4
 MESH = pl.DeviceIdType.MESH
 
 cheb_shift = 3.75
@@ -135,34 +136,50 @@
     def turned(value):
         return jnp.swapaxes(value.astype(jnp.float32), 0, 1)
 
-    def advance(k, q, c, b):
+    def advance(count, k, q, c, b):
         source = fields[k - 1]
-        values = [source[q, :, pl.ds(i * LANES, LANES)] for i in range(cols)]
-        ups = [pltpu.roll(v, LANES - NZ, 1) for v in values]
-        downs = [pltpu.roll(v, NZ, 1) for v in values]
         zero = jnp.zeros((ROWS, LANES), jnp.float32)
+
+        def rotate(i):
+            at = pl.ds(i * LANES, LANES)
+            ups, downs, sides = [], [], []
+            for u in range(count):
+                v = source[q + u, :, at]
+                ups.append(pltpu.roll(v, LANES - NZ, 1))
+                downs.append(pltpu.roll(v, NZ, 1))
+                upper_z = jnp.where(z_pos < NZ - 1, pltpu.roll(v, LANES - 1, 1), 0.0)
+                lower_z = jnp.where(z_pos > 0, pltpu.roll(v, 1, 1), 0.0)
+                sides.append(upper_z + lower_z)
+            return ups, downs, sides
+
+        nothing = ([zero] * count,) * 3
+        before, here = nothing, rotate(0)
         for i in range(cols):
+            after = rotate(i + 1) if i + 1 < cols else nothing
             at = pl.ds(i * LANES, LANES)
-            v = values[i]
-            upper_z = jnp.where(z_pos < NZ - 1, pltpu.roll(v, LANES - 1, 1), 0.0)
-            lower_z = jnp.where(z_pos > 0, pltpu.roll(v, 1, 1), 0.0)
-            upper_y = jnp.where(lane < LANES - NZ, ups[i], ups[i + 1] if i + 1 < cols else zero)
-            lower_y = jnp.where(lane >= NZ, downs[i], downs[i - 1] if i else zero)
-            beside = (source[q + 1, :, at] + source[q - 1, :, at]) + (upper_y + lower_y)
-            beside = beside + (upper_z + lower_z)
-            a8 = alpha[q, :, at]
-            applied = jnp.concatenate([a8] * (ROWS // 8), axis=0) * v - beside
-            if k == 1:
-                result = applied * (0.5 / cheb_scale)
-            else:
-                result = applied * (1.0 / cheb_scale) - fields[k - 2][q, :, at]
-            if k < DEGREE:
-                fields[k][q, :, at] = result
-            else:
-                offset = (q - DEGREE - b * block) * width + i * LANES
-                stage[c, b, :, pl.ds(pl.multiple_of(offset, LANES), LANES)] = result.astype(
-                    jnp.bfloat16
-                )
+            line = [source[q + u - 1, :, at] for u in range(count + 2)]
+            results = []
+            for u in range(count):
+                upper_y = jnp.where(lane < LANES - NZ, here[0][u], after[0][u])
+                lower_y = jnp.where(lane >= NZ, here[1][u], before[1][u])
+                beside = (line[u + 2] + line[u]) + (upper_y + lower_y)
+                beside = beside + here[2][u]
+                a8 = alpha[q + u, :, at]
+                applied = jnp.concatenate([a8] * (ROWS // 8), axis=0) * line[u + 1] - beside
+                if k == 1:
+                    result = applied * (0.5 / cheb_scale)
+                else:
+                    result = applied * (1.0 / cheb_scale) - fields[k - 2][q + u, :, at]
+                results.append(result)
+            for u in range(count):
+                if k < DEGREE:
+                    fields[k][q + u, :, at] = results[u]
+                else:
+                    offset = (q + u - DEGREE - b * block) * width + i * LANES
+                    stage[c, b, :, pl.ds(pl.multiple_of(offset, LANES), LANES)] = results[
+                        u
+                    ].astype(jnp.bfloat16)
+            before, here = here, after
 
     def send_copy(c, b):
         return pltpu.make_async_remote_copy(
@@ -260,11 +277,18 @@
                     high, jnp.where(has_next, planes + DEGREE + reach, planes + DEGREE)
                 )
 
+                groups = jnp.maximum(high - low, 0) // GROUP
+
+                def group_body(t, nothing):
+                    advance(GROUP, k, low + t * GROUP, c, b)
+                    return nothing
+
                 def plane_body(q, nothing):
-                    advance(k, q, c, b)
+                    advance(1, k, q, c, b)
                     return nothing
 
-                lax.fori_loop(low, high, plane_body, 0)
+                lax.fori_loop(0, groups, group_body, 0)
+                lax.fori_loop(low + groups * GROUP, high, plane_body, 0)
 
             if chunks == 1:
                 issue(c, b)

time: 212 us -> 207 us (0.976)
  Pallas kernels: 212 us -> 206 us
    pallas_call x1, Pallas kernels: 201 us -> 195 us  [local(): pl.pallas_call(functools.partial(filter_kernel, n_dom, n_st, parts), out_...]
where the time goes in v4:
time: 207 us; the launch traced here: 206 us
  Pallas kernels  206 us (100%)
    pallas_call x1, Pallas kernels, local(): pl.pallas_call(functools.partial(filter_kernel, n_dom, n_st, parts), out_...  195 us
    pallas_call x1, Pallas kernels, local(): pl.pallas_call(rotate_kernel, out_shape=jax.ShapeDtypeStruct((n_st * stat...  11 us

profile of v4, /device:TPU:0, one launch (start us, length us, event | category | flops | bytes accessed | tf_op | source)
XLA Modules:
  0.0 205.9 jit_solution(15174162376666234898)
XLA Ops:
  0.0 194.9 %filter_exchange.1 = (bf16[512,8192]{1,0:T(8,128)(2,1)}, bf16[8,4,16,512]{3,2,1,0:T(8,128)(2,1)}) custom-call(bf16[64,64,1024]{2,1,0:T(8,128)(2,1)} %orb.1, bf16[64,1024]{1,0:T(8,128)(2,1)} %pot.1, bf16[64,512]{1,0:T(8,128)(2,1)} %rot.1), custom_call_target="tpu_custom_call" | custom-call | flops 218103808 | bytes 16777216 | tf_op jit(solution)/shard_map/filter_exchange/pallas_call | solution.py:382
  194.9 11.0 %rotate.1 = bf16[512,8192]{1,0:T(8,128)(2,1)} custom-call(bf16[512,512]{1,0:T(8,128)(2,1)} %bitcast.1, bf16[512,8192]{1,0:T(8,128)(2,1)} %get-tuple-element.8.states), custom_call_target="tpu_custom_call" | custom-call | flops 4294967296 | bytes 16777216 | tf_op jit(solution)/shard_map/rotate/pallas_call | solution.py:415
